TPU v7x, 128 devices: a whole 4x4x4 slice. The times are simulated.
128 devices in a mesh: str: 16 (over x_lo, y, core), crs: 8 (over x_hi, z).
Axes of the slice: x: 4 (x_hi: 2, x_lo: 2; x = x_hi * 2 + x_lo), y: 4, z: 4, core: 2. Of those that a mesh axis runs over, the one named last changes fastest.
Arguments:
- voltage: float32 [4, 512, 16384], P(None, 'str', 'crs'), may hold values from -4 to 0.5
- photocurrent: float32 [4, 512, 16384], P(None, 'str', 'crs'), may hold values from 0.1 to 10
- shunt: float32 [512, 16384], P('str', 'crs'), may hold values from 0.02 to 0.5
- series: float32 [512, 16384], P('str', 'crs'), may hold values from 0.5 to 2
- pattern: int32 [512, 128], P('str', 'crs'), may hold values from 0 to 3
- diode_mask: int32 [512, 128], P('str', 'crs'), may hold values 0 or 1
- aggregate: int32 [512, 128], P('str', 'crs'), may hold values from 0 to 4095, as said below
- coarse_inverse: float32 [4096, 4096], P('crs'), as said below
Outputs:
- newton_step: float32 [4, 512, 16384], P(None, 'str', 'crs')
- residual: float32 [4, 512, 16384], P(None, 'str', 'crs')
Inputs may be any that keep to these rules, and one draw needn't show every extreme that they name: `aggregate`: every value appears. coarse_inverse is symmetric positive definite.
All inputs are finite; a program needn't handle non-finite values. No bound on the sum of `diode_mask` on one device may be relied on, other than what follows from the above.
Results may differ from a plain program's by a relative error of at most 0.0003.
Values sent between devices are 32-bit elements; how exact they have to be, the bound alone decides.
A program may use at most 64 MiB of HBM per device.

v0:
```python
import jax
import jax.numpy as jnp
from jax import lax
from jax.sharding import PartitionSpec as P

ITERS = 3
LEVELS = (0.25, 0.5, 1.0, 2.0)
DIODE_SAT = 0.5


def with_halo(block, sides, width, periodic):
    for axis, dim in sides:
        count = lax.axis_size(axis)
        forward = [(i, i + 1) for i in range(count - 1)]
        if periodic:
            forward.append((count - 1, 0))
        backward = [(target, source) for source, target in forward]
        low = lax.ppermute(
            lax.slice_in_dim(block, block.shape[dim] - width, None, axis=dim), axis, forward
        )
        high = lax.ppermute(lax.slice_in_dim(block, 0, width, axis=dim), axis, backward)
        block = jnp.concatenate([low, block, high], axis=dim)
    return block


def widen(blocks):
    shape = blocks.shape
    spread = jnp.broadcast_to(blocks[..., None], shape + (128,))
    return spread.reshape(shape[:-1] + (shape[-1] * 128,))


def cross_levels(pattern):
    total = jnp.zeros(pattern.shape, jnp.float32)
    for number in range(4):
        total = total + jnp.where(pattern == number, jnp.float32(LEVELS[number]), jnp.float32(0.0))
    return total


def neighbours(field):
    along = with_halo(field, (("str", 1),), 1, True)
    across = with_halo(field, (("crs", 2),), 1, False)
    return (along[:, 2:], along[:, :-2], across[:, :, 2:], across[:, :, :-2])


def shards(voltage, photocurrent, shunt, series, pattern, diode_mask, aggregate, coarse_inverse):
    points = voltage.shape[0]
    rows_here = voltage.shape[1]
    local_block_list = voltage.shape[2] // 128
    coarse_count = coarse_inverse.shape[1]
    cross_level = widen(cross_levels(pattern))
    diode_area = widen(diode_mask.astype(jnp.float32))
    flat_groups = aggregate.reshape(-1)
    stacked = jnp.concatenate([voltage, cross_level[None], series[None]], axis=0)
    below, above, right_cells, left_cells = neighbours(stacked)
    right_link = jnp.minimum(cross_level, right_cells[points])
    left_link = jnp.minimum(cross_level, left_cells[points])
    up_link = above[points + 1]
    diode_derivative = DIODE_SAT * diode_area * jnp.exp(voltage)
    imbalance = (
        shunt * voltage
        + series * (voltage - below[:points])
        + up_link * (voltage - above[:points])
        + right_link * (voltage - right_cells[:points])
        + left_link * (voltage - left_cells[:points])
        + diode_derivative
        - DIODE_SAT * diode_area
        - photocurrent
    )
    diagonal = shunt + diode_derivative + series + up_link + right_link + left_link

    def restrict(remainder):
        block_sums = remainder.reshape(points, rows_here * local_block_list, 128).sum(axis=-1)
        return jax.ops.segment_sum(block_sums.T, flat_groups, num_segments=coarse_count).T

    def interpolate_upward(correction):
        picked = jnp.take(correction, flat_groups, axis=1)
        return widen(picked.reshape(points, rows_here, local_block_list))

    def coarse_solve(incomplete_value):
        product = None
        total = lax.psum(incomplete_value, ("str", "crs"))
        row_share = lax.dot_general(
            total, coarse_inverse, (((1,), (1,)), ((), ())), precision=lax.Precision.HIGHEST
        )
        correction = lax.all_gather(row_share, "crs", axis=1, tiled=True)
        return (correction, product)

    def precondition(remainder):
        resident_portion = remainder / diagonal
        incomplete_value = restrict(remainder)
        correction, product = coarse_solve(incomplete_value)
        smoothed = resident_portion + interpolate_upward(correction)
        product = lax.psum(jnp.sum(remainder * smoothed, axis=(1, 2)), ("str", "crs"))
        return (smoothed, product)

    remainder = -imbalance
    newton_step = jnp.zeros_like(voltage)
    smoothed, product = precondition(remainder)
    direction = smoothed
    for turn in range(ITERS):
        operate_below, operate_above, operate_right_cells, operate_left_cells = neighbours(
            direction
        )
        image = (
            diagonal * direction
            - series * operate_below
            - up_link * operate_above
            - right_link * operate_right_cells
            - left_link * operate_left_cells
        )
        curvature = lax.psum(jnp.sum(direction * image, axis=(1, 2)), ("str", "crs"))
        alpha = (product / curvature)[:, None, None]
        newton_step = newton_step + alpha * direction
        remainder = remainder - alpha * image
        if turn + 1 < ITERS:
            smoothed, fresh = precondition(remainder)
            ratio = (fresh / product)[:, None, None]
            direction = smoothed + ratio * direction
            product = fresh
    return (newton_step, remainder)


def solution(mesh):
    placed = (
        P(None, "str", "crs"),
        P(None, "str", "crs"),
        P("str", "crs"),
        P("str", "crs"),
        P("str", "crs"),
        P("str", "crs"),
        P("str", "crs"),
        P("crs", None),
    )
    return jax.shard_map(
        shards,
        mesh=mesh,
        in_specs=placed,
        out_specs=(P(None, "str", "crs"), P(None, "str", "crs")),
        check_vma=False,
    )
```

profile of v0, /device:TPU:1, one launch (start us, length us, event | category | flops | bytes accessed | tf_op | source)
XLA Modules:
  0.0 1062.8 jit_solution(3380685636923150555)
XLA Ops:
  9.5 1.5 collective-permute-start
  11.0 1.3 collective-permute-start.1
  13.7 4.2 collective-permute-start.3
  20.6 2.9 fusion.30
  24.8 1.6 reduce_sum.81
  26.5 3.8 scatter_custom_fusion
  30.4 158.7 %all-reduce.5.cloned.1.call-done = f32[4,4096]{0,1:T(8,128)} async-done(((f32[4,4096]{0,1:T(8,128)}), f32[4,4096]{0,1:T(8,128)}) %all-reduce.5.cloned.1.call-update) | async-done | bytes 65552 | tf_op jit(solution)/shard_map/psum | solution.py:81
  189.0 10.9 %fusion.54 = f32[4,512]{1,0:T(4,128)S(1)} fusion(f32[4,4096]{0,1:T(8,128)} %all-reduce.5.cloned.1.call-done, f32[512,4096]{1,0:T(8,128)} %param.17), kind=kOutput, calls=%fused_computation.118 | convolution fusion | flops 100663296 | bytes 8462336 | tf_op jit(solution)/shard_map/dot_general | solution.py:82
  199.9 28.1 %all_gather.9 = f32[4,4096]{1,0:T(4,128)S(1)} all-gather(f32[4,512]{1,0:T(4,128)S(1)} %fusion.54), channel_id=1, replica_groups=mesh['str'=16,'crs'=8] {'crs'}, dimensions={1}, use_global_device_ids=true | all-gather | bytes 73728 | tf_op jit(solution)/shard_map/all_gather | solution.py:85
  228.7 1.6 gather_fusion
  233.2 2.6 divide_add_fusion.2
  235.8 7.2 collective-permute-start.4
  245.6 4.0 collective-permute-start.7
  249.7 1.8 collective-permute-done.7
  252.5 69.2 %all-reduce = (f32[4]{0:T(128)}, f32[4]{0:T(128)}) all-reduce(f32[4]{0:T(128)S(1)} %get-tuple-element.4, f32[4]{0:T(128)S(1)} %get-tuple-element.3), channel_id=1, replica_groups=mesh['str'=16,'crs'=8] {'str','crs'}, use_global_device_ids=true, to_apply=%region_4.6 | all-reduce | flops 8 | bytes 64 | tf_op jit(solution)/shard_map/psum | solution.py:93
  322.4 2.8 multiply_subtract_fusion.2
  325.2 1.4 reshape.56
  327.1 3.8 scatter_custom_fusion.1
  331.1 147.5 %all-reduce.7.cloned.1.call-done = f32[4,4096]{0,1:T(8,128)} async-done(((f32[4,4096]{0,1:T(8,128)}), f32[4,4096]{0,1:T(8,128)}) %all-reduce.7.cloned.1.call-update) | async-done | bytes 65552 | tf_op jit(solution)/shard_map/psum | solution.py:81
  478.6 10.9 %fusion.55 = f32[4,512]{1,0:T(4,128)S(1)} fusion(f32[4,4096]{0,1:T(8,128)} %all-reduce.7.cloned.1.call-done, f32[512,4096]{1,0:T(8,128)} %param.17), kind=kOutput, calls=%fused_computation.119 | convolution fusion | flops 100663296 | bytes 8462336 | tf_op jit(solution)/shard_map/dot_general | solution.py:82
  489.4 27.8 %all_gather.10 = f32[4,4096]{1,0:T(4,128)S(1)} all-gather(f32[4,512]{1,0:T(4,128)S(1)} %fusion.55), channel_id=1, replica_groups=mesh['str'=16,'crs'=8] {'crs'}, dimensions={1}, use_global_device_ids=true | all-gather | bytes 73728 | tf_op jit(solution)/shard_map/all_gather | solution.py:85
  517.2 2.0 copy.34
  519.2 3.3 gather_fusion.1
  522.6 1.8 broadcast_select_fusion.1
  526.9 2.4 reshape.57
  529.3 1.6 multiply_reduce_fusion.3
  530.8 70.0 %psum.67 = f32[4]{0:T(128)S(1)} all-reduce(f32[4]{0:T(128)S(1)} %multiply_reduce_fusion.3), channel_id=1, replica_groups=mesh['str'=16,'crs'=8] {'str','crs'}, use_global_device_ids=true, to_apply=%region_11.13 | all-reduce | flops 4 | bytes 32 | tf_op jit(solution)/shard_map/psum | solution.py:93
  600.8 1.9 multiply_add_fusion.2
  606.0 4.0 collective-permute-start.11
  613.3 71.4 %psum.68 = f32[4]{0:T(128)} all-reduce(f32[4]{0:T(128)S(1)} %multiply_reduce_fusion.2), channel_id=1, replica_groups=mesh['str'=16,'crs'=8] {'str','crs'}, use_global_device_ids=true, to_apply=%region_13.15 | all-reduce | flops 4 | bytes 32 | tf_op jit(solution)/shard_map/psum | solution.py:111
  685.4 3.1 multiply_subtract_fusion.1
  688.5 2.4 reshape.58
  690.8 1.6 reduce_sum.87
  693.3 4.1 scatter_custom_fusion.2
  697.3 147.4 %all-reduce.9.cloned.1.call-done = f32[4,4096]{0,1:T(8,128)} async-done(((f32[4,4096]{0,1:T(8,128)}), f32[4,4096]{0,1:T(8,128)}) %all-reduce.9.cloned.1.call-update) | async-done | bytes 65552 | tf_op jit(solution)/shard_map/psum | solution.py:81
  844.8 10.9 %fusion.56 = f32[4,512]{1,0:T(4,128)S(1)} fusion(f32[4,4096]{0,1:T(8,128)} %all-reduce.9.cloned.1.call-done, f32[512,4096]{1,0:T(8,128)} %param.17), kind=kOutput, calls=%fused_computation.120 | convolution fusion | flops 100663296 | bytes 8462336 | tf_op jit(solution)/shard_map/dot_general | solution.py:82
  855.6 27.8 %all_gather.11 = f32[4,4096]{1,0:T(4,128)S(1)} all-gather(f32[4,512]{1,0:T(4,128)S(1)} %fusion.56), channel_id=1, replica_groups=mesh['str'=16,'crs'=8] {'crs'}, dimensions={1}, use_global_device_ids=true | all-gather | bytes 73728 | tf_op jit(solution)/shard_map/all_gather | solution.py:85
  883.4 2.0 copy.37
  885.4 3.2 gather_fusion.2
  888.6 1.8 broadcast_select_fusion
  893.0 2.4 reshape.59
  895.4 1.9 multiply_reduce_fusion.1
  897.2 70.1 %psum.70 = f32[4]{0:T(128)S(1)} all-reduce(f32[4]{0:T(128)S(1)} %multiply_reduce_fusion.1), channel_id=1, replica_groups=mesh['str'=16,'crs'=8] {'str','crs'}, use_global_device_ids=true, to_apply=%region_18.20 | all-reduce | flops 4 | bytes 32 | tf_op jit(solution)/shard_map/psum | solution.py:93
  967.4 1.9 multiply_add_fusion.1
  972.6 4.0 collective-permute-start.15
  979.9 71.0 %psum.71 = f32[4]{0:T(128)} all-reduce(f32[4]{0:T(128)S(1)} %multiply_reduce_fusion), channel_id=1, replica_groups=mesh['str'=16,'crs'=8] {'str','crs'}, use_global_device_ids=true, to_apply=%region_20.22 | all-reduce | flops 4 | bytes 32 | tf_op jit(solution)/shard_map/psum | solution.py:111
  1051.6 2.7 multiply_add_fusion
  1054.3 1.7 multiply_subtract_fusion
  (160 shorter events, 36.8 us)
Async XLA Ops:
  7.2 5.2 copy-start.1
  7.2 5.1 copy-start
  7.2 181.9 %all-reduce.5.cloned.1.call-start = ((), (), s32[]{:S(2)}) async-start(), calls=%async_computation | async-start | bytes 4194304 | tf_op jit(solution)/shard_map/psum | solution.py:81
  8.1 9.8 copy-start.39
  8.1 9.8 copy-start.37
  9.5 10.3 collective-permute-start
  11.0 8.6 collective-permute-start.1
  12.4 7.1 collective-permute-start.2
  13.7 5.8 collective-permute-start.3
  19.8 3.7 copy-start.7
  19.8 3.7 copy-start.12
  19.8 3.7 copy-start.17
  23.5 6.8 copy-start.3
  26.5 3.9 copy-start.38
  30.3 448.3 %all-reduce.7.cloned.1.call-start = ((), (), s32[]{:S(2)}) async-start(), calls=%async_computation.1 | async-start | bytes 4194304 | tf_op jit(solution)/shard_map/psum | solution.py:81
  199.9 30.4 %copy-start.36 = (pred[512]{0:T(512)(128)(4,1)S(1)}, pred[512]{0:T(512)(128)(4,1)}, u32[]{:S(2)}) copy-start(pred[512]{0:T(512)(128)(4,1)} %compare_and_fusion) | copy-start | bytes 1540
  233.2 18.4 %copy-start.4 = (f32[4,32,2048]{2,1,0:T(8,128)S(1)}, f32[4,32,2048]{2,1,0:T(8,128)}, u32[]{:S(2)}) copy-start(f32[4,32,2048]{2,1,0:T(8,128)} %copy-done.3) | copy-start | bytes 3145732
  233.2 18.4 %copy-start.8 = (f32[32,2048]{1,0:T(8,128)S(1)}, f32[32,2048]{1,0:T(8,128)}, u32[]{:S(2)}) copy-start(f32[32,2048]{1,0:T(8,128)} %copy-done.7) | copy-start | bytes 786436
  233.2 18.4 %copy-start.13 = (f32[32,2048]{1,0:T(8,128)S(1)}, f32[32,2048]{1,0:T(8,128)}, u32[]{:S(2)}) copy-start(f32[32,2048]{1,0:T(8,128)} %copy-done.12) | copy-start | bytes 786436
  233.2 18.4 %copy-start.18 = (f32[32,2048]{1,0:T(8,128)S(1)}, f32[32,2048]{1,0:T(8,128)}, u32[]{:S(2)}) copy-start(f32[32,2048]{1,0:T(8,128)} %copy-done.17) | copy-start | bytes 786436
  235.8 15.7 %collective-permute-start.4 = (f32[4,1,2048]{2,1,0:T(1,128)S(1)}, f32[4,1,2048]{2,1,0:T(1,128)S(1)}, u32[]{:S(2)}, u32[]{:S(2)}) collective-permute-start(f32[4,1,2048]{2,1,0:T(1,128)S(1)} %get-tuple-element.24), channel_id=1, source_target_pairs={{8,0},{16,8},{24,16},{32,24},{40,32},{48,40},{56,48},{64,56},{72,6... | collective-permute-start | bytes 98312 | tf_op jit(solution)/shard_map/ppermute | solution.py:21
  243.0 8.6 collective-permute-start.5
  244.3 5.4 collective-permute-start.6
  245.6 5.9 collective-permute-start.7
  251.6 70.8 %copy-start.5 = (f32[4,32,2048]{2,1,0:T(8,128)S(1)}, f32[4,32,2048]{2,1,0:T(8,128)}, u32[]{:S(2)}) copy-start(f32[4,32,2048]{2,1,0:T(8,128)} %copy-done.3) | copy-start | bytes 3145732
  330.9 513.9 %all-reduce.9.cloned.1.call-start = ((), (), s32[]{:S(2)}) async-start(), calls=%async_computation.2 | async-start | bytes 4194304 | tf_op jit(solution)/shard_map/psum | solution.py:81
  519.2 10.0 copy-start.6
  529.3 71.5 %copy-start.42 = (f32[4]{0:T(128)S(1)}, f32[4]{0:T(128)}, u32[]{:S(2)}) copy-start(f32[4]{0:T(128)} %get-tuple-element.5) | copy-start | bytes 52
  600.8 11.7 %copy-start.9 = (f32[32,2048]{1,0:T(8,128)S(1)}, f32[32,2048]{1,0:T(8,128)}, u32[]{:S(2)}) copy-start(f32[32,2048]{1,0:T(8,128)} %copy-done.7) | copy-start | bytes 786436
  600.8 11.7 %copy-start.14 = (f32[32,2048]{1,0:T(8,128)S(1)}, f32[32,2048]{1,0:T(8,128)}, u32[]{:S(2)}) copy-start(f32[32,2048]{1,0:T(8,128)} %copy-done.12) | copy-start | bytes 786436
  600.8 11.7 %copy-start.19 = (f32[32,2048]{1,0:T(8,128)S(1)}, f32[32,2048]{1,0:T(8,128)}, u32[]{:S(2)}) copy-start(f32[32,2048]{1,0:T(8,128)} %copy-done.17) | copy-start | bytes 786436
  602.8 8.5 collective-permute-start.8
  604.0 7.3 collective-permute-start.9
  604.7 5.7 collective-permute-start.10
  606.0 5.3 collective-permute-start.11
  895.4 72.0 %copy-start.41 = (f32[4]{0:T(128)S(1)}, f32[4]{0:T(128)}, u32[]{:S(2)}) copy-start(f32[4]{0:T(128)} %copy-done.40) | copy-start | bytes 52
  967.4 11.7 %copy-start.10 = (f32[32,2048]{1,0:T(8,128)S(1)}, f32[32,2048]{1,0:T(8,128)}, u32[]{:S(2)}) copy-start(f32[32,2048]{1,0:T(8,128)} %copy-done.7) | copy-start | bytes 786436
  967.4 11.7 %copy-start.15 = (f32[32,2048]{1,0:T(8,128)S(1)}, f32[32,2048]{1,0:T(8,128)}, u32[]{:S(2)}) copy-start(f32[32,2048]{1,0:T(8,128)} %copy-done.12) | copy-start | bytes 786436
  967.4 11.7 %copy-start.20 = (f32[32,2048]{1,0:T(8,128)S(1)}, f32[32,2048]{1,0:T(8,128)}, u32[]{:S(2)}) copy-start(f32[32,2048]{1,0:T(8,128)} %copy-done.17) | copy-start | bytes 786436
  969.3 8.6 copy-start.22
  969.4 8.5 collective-permute-start.12
  970.5 7.3 collective-permute-start.13
  971.3 5.7 collective-permute-start.14
  972.6 5.3 collective-permute-start.15
  1051.6 2.7 copy-start.21
  1051.6 2.7 copy-start.23
  1051.6 2.7 copy-start.27
  1051.6 2.7 copy-start.30
  (14 other events, 17.6 us)
Sparse Core Ops, SparseCore 0:
  30.4 158.5 all-reduce.4
  331.0 147.5 all-reduce.6
  697.5 147.2 all-reduce.8
where the time goes:
time: 1070 us; the launch traced here: 1060 us
  waiting for transfers between devices  458 us (43%)
  blocking collectives  435 us (41%)
  other arithmetic  50.6 us (5%)
  starting transfers between devices  36.5 us (3%)
  local copies, waits for them, and re-layouts  35 us (3%)
  matrix products  32.6 us (3%)
  between operations  14.5 us (1%)
    psum x3, waiting for transfers between devices, coarse_solve(): total = lax.psum(incomplete_value, ('str', 'crs'))  454 us
    psum x3, blocking collectives, precondition(): lax.psum(jnp.sum(remainder * smoothed, axis=(1, 2)), ('str', 'crs'))  209 us
    psum x2, blocking collectives, shards(): lax.psum(jnp.sum(direction * image, axis=(1, 2)), ('str', 'crs'))  142 us
    all_gather x3, blocking collectives, coarse_solve(): correction = lax.all_gather(row_share, 'crs', axis=1, tiled=True)  83.8 us
    dot_general x3, matrix products, coarse_solve(): lax.dot_general(total, coarse_inverse, (((1,), (1,)), ((), ())), precisio...  32.6 us
  transfers between devices with their start and end apart: 19, of which 9 were waited for; matrix products, arithmetic and copies ran while one was open for 0% of the time, Pallas kernels for 0%

commit v1 on v0

--- a/solution.py
+++ b/solution.py
@@ -78,7 +78,13 @@
 
     def coarse_solve(incomplete_value):
         product = None
-        total = lax.psum(incomplete_value, ("str", "crs"))
+
+        def _switch_table(z):
+            for dd in ("str", "crs"):
+                z = jax.lax.psum(z, dd)
+            return z
+
+        total = _switch_table(incomplete_value)
         row_share = lax.dot_general(
             total, coarse_inverse, (((1,), (1,)), ((), ())), precision=lax.Precision.HIGHEST
         )

time: 1070 us -> 1280 us (1.20)
  waiting for transfers between devices: 458 us -> 650 us
    psum x3 -> x6, waiting for transfers between devices: 454 us -> 646 us  [_switch_table(): z = jax.lax.psum(z, dd)]
  transfers between devices with their start and end apart: 19 -> 22, of which waited for: 9 -> 10; matrix products, arithmetic and copies ran while one was open for 0% -> 0% of each run, Pallas kernels for 0% -> 0%
where the time goes in v1:
time: 1280 us; the launch traced here: 1270 us
  waiting for transfers between devices  650 us (51%)
  blocking collectives  444 us (35%)
  other arithmetic  50.9 us (4%)
  starting transfers between devices  41.1 us (3%)
  local copies, waits for them, and re-layouts  36 us (3%)
  matrix products  32.6 us (3%)
  between operations  14.9 us (1%)
    psum x6, waiting for transfers between devices, _switch_table(): z = jax.lax.psum(z, dd)  646 us
    psum x3, blocking collectives, precondition(): lax.psum(jnp.sum(remainder * smoothed, axis=(1, 2)), ('str', 'crs'))  217 us
    psum x2, blocking collectives, shards(): lax.psum(jnp.sum(direction * image, axis=(1, 2)), ('str', 'crs'))  143 us
    all_gather x3, blocking collectives, coarse_solve(): correction = lax.all_gather(row_share, 'crs', axis=1, tiled=True)  84.1 us
    dot_general x3, matrix products, coarse_solve(): lax.dot_general(total, coarse_inverse, (((1,), (1,)), ((), ())), precisio...  32.6 us
  transfers between devices with their start and end apart: 22, of which 10 were waited for; matrix products, arithmetic and copies ran while one was open for 0% of the time, Pallas kernels for 0%

profile of v1, /device:TPU:1, one launch (start us, length us, event | category | flops | bytes accessed | tf_op | source)
XLA Modules:
  0.0 1269.7 jit_solution(911459735426293775)
XLA Ops:
  13.7 4.2 collective-permute-start.3
  20.6 2.9 fusion.30
  24.8 1.6 reduce_sum.81
  26.5 3.6 scatter_custom_fusion
  30.3 130.9 %all-reduce.8.cloned.1.call-done = f32[4,4096]{0,1:T(8,128)} async-done(((f32[4,4096]{0,1:T(8,128)}), f32[4,4096]{0,1:T(8,128)}) %all-reduce.8.cloned.1.call-update) | async-done | bytes 65552 | tf_op jit(solution)/shard_map/psum | solution.py:84
  161.3 91.9 %all-reduce.10.cloned.1.call-done = f32[4,4096]{0,1:T(8,128)} async-done(((f32[4,4096]{0,1:T(8,128)}), f32[4,4096]{0,1:T(8,128)}) %all-reduce.10.cloned.1.call-update) | async-done | bytes 65552 | tf_op jit(solution)/shard_map/psum | solution.py:84
  253.1 10.9 fusion.54
  264.0 28.2 %all_gather.9 = f32[4,4096]{1,0:T(4,128)S(1)} all-gather(f32[4,512]{1,0:T(4,128)S(1)} %fusion.54), channel_id=1, replica_groups=mesh['str'=16,'crs'=8] {'crs'}, dimensions={1}, use_global_device_ids=true | all-gather | bytes 73728 | tf_op jit(solution)/shard_map/all_gather | solution.py:91
  292.8 1.6 gather_fusion
  297.3 2.6 divide_add_fusion.2
  299.9 11.7 collective-permute-start.4
  314.2 4.0 collective-permute-start.7
  318.5 1.5 collective-permute-done.7
  321.5 69.7 %all-reduce = (f32[4]{0:T(128)}, f32[4]{0:T(128)}) all-reduce(f32[4]{0:T(128)} %get-tuple-element.4, f32[4]{0:T(128)S(1)} %get-tuple-element.3), channel_id=1, replica_groups=mesh['str'=16,'crs'=8] {'str','crs'}, use_global_device_ids=true, to_apply=%region_5.7 | all-reduce | flops 8 | bytes 64 | tf_op jit(solution)/shard_map/psum | solution.py:99
  391.8 2.8 multiply_subtract_fusion.2
  396.5 3.6 scatter_custom_fusion.1
  400.2 119.9 %all-reduce.12.cloned.1.call-done = f32[4,4096]{0,1:T(8,128)} async-done(((f32[4,4096]{0,1:T(8,128)}), f32[4,4096]{0,1:T(8,128)}) %all-reduce.12.cloned.1.call-update) | async-done | bytes 65552 | tf_op jit(solution)/shard_map/psum | solution.py:84
  520.4 91.5 %all-reduce.14.cloned.1.call-done = f32[4,4096]{0,1:T(8,128)} async-done(((f32[4,4096]{0,1:T(8,128)}), f32[4,4096]{0,1:T(8,128)}) %all-reduce.14.cloned.1.call-update) | async-done | bytes 65552 | tf_op jit(solution)/shard_map/psum | solution.py:84
  611.9 10.9 fusion.55
  622.8 28.0 %all_gather.10 = f32[4,4096]{1,0:T(4,128)S(1)} all-gather(f32[4,512]{1,0:T(4,128)S(1)} %fusion.55), channel_id=1, replica_groups=mesh['str'=16,'crs'=8] {'crs'}, dimensions={1}, use_global_device_ids=true | all-gather | bytes 73728 | tf_op jit(solution)/shard_map/all_gather | solution.py:91
  650.8 2.0 copy.34
  652.7 3.3 gather_fusion.1
  656.1 1.8 broadcast_select_fusion.1
  660.4 2.4 reshape.57
  662.8 1.6 multiply_reduce_fusion.3
  664.4 73.7 %psum.90 = f32[4]{0:T(128)S(1)} all-reduce(f32[4]{0:T(128)S(1)} %multiply_reduce_fusion.3), channel_id=1, replica_groups=mesh['str'=16,'crs'=8] {'str','crs'}, use_global_device_ids=true, to_apply=%region_13.15 | all-reduce | flops 4 | bytes 32 | tf_op jit(solution)/shard_map/psum | solution.py:99
  738.1 1.9 multiply_add_fusion.2
  743.3 4.0 collective-permute-start.11
  751.1 71.5 %psum.91 = f32[4]{0:T(128)} all-reduce(f32[4]{0:T(128)} %multiply_reduce_fusion.2), channel_id=1, replica_groups=mesh['str'=16,'crs'=8] {'str','crs'}, use_global_device_ids=true, to_apply=%region_15.17 | all-reduce | flops 4 | bytes 32 | tf_op jit(solution)/shard_map/psum | solution.py:117
  823.8 3.1 multiply_subtract_fusion.1
  826.9 2.4 reshape.58
  829.3 1.6 reduce_sum.87
  831.7 4.0 scatter_custom_fusion.2
  835.8 119.8 %all-reduce.16.cloned.1.call-done = f32[4,4096]{0,1:T(8,128)} async-done(((f32[4,4096]{0,1:T(8,128)}), f32[4,4096]{0,1:T(8,128)}) %all-reduce.16.cloned.1.call-update) | async-done | bytes 65552 | tf_op jit(solution)/shard_map/psum | solution.py:84
  955.6 91.8 %all-reduce.18.cloned.1.call-done = f32[4,4096]{0,1:T(8,128)} async-done(((f32[4,4096]{0,1:T(8,128)}), f32[4,4096]{0,1:T(8,128)}) %all-reduce.18.cloned.1.call-update) | async-done | bytes 65552 | tf_op jit(solution)/shard_map/psum | solution.py:84
  1047.4 10.9 fusion.56
  1058.3 28.0 %all_gather.11 = f32[4,4096]{1,0:T(4,128)S(1)} all-gather(f32[4,512]{1,0:T(4,128)S(1)} %fusion.56), channel_id=1, replica_groups=mesh['str'=16,'crs'=8] {'crs'}, dimensions={1}, use_global_device_ids=true | all-gather | bytes 73728 | tf_op jit(solution)/shard_map/all_gather | solution.py:91
  1086.2 2.0 copy.37
  1088.2 3.2 gather_fusion.2
  1091.4 1.8 broadcast_select_fusion
  1095.8 2.4 reshape.59
  1098.2 1.9 multiply_reduce_fusion.1
  1100.1 73.9 %psum.94 = f32[4]{0:T(128)S(1)} all-reduce(f32[4]{0:T(128)S(1)} %multiply_reduce_fusion.1), channel_id=1, replica_groups=mesh['str'=16,'crs'=8] {'str','crs'}, use_global_device_ids=true, to_apply=%region_21.23 | all-reduce | flops 4 | bytes 32 | tf_op jit(solution)/shard_map/psum | solution.py:99
  1173.9 1.9 multiply_add_fusion.1
  1179.1 4.0 collective-permute-start.15
  1186.5 71.1 %psum.95 = f32[4]{0:T(128)} all-reduce(f32[4]{0:T(128)S(1)} %multiply_reduce_fusion), channel_id=1, replica_groups=mesh['str'=16,'crs'=8] {'str','crs'}, use_global_device_ids=true, to_apply=%region_23.25 | all-reduce | flops 4 | bytes 32 | tf_op jit(solution)/shard_map/psum | solution.py:117
  1258.2 2.7 multiply_add_fusion
  1260.9 1.7 multiply_subtract_fusion
  (173 shorter events, 42.9 us)
Async XLA Ops:
  7.2 5.2 copy-start.1
  7.2 5.1 copy-start
  7.2 154.0 %all-reduce.8.cloned.1.call-start = ((), (), s32[]{:S(2)}) async-start(), calls=%async_computation | async-start | bytes 4194304 | tf_op jit(solution)/shard_map/psum | solution.py:84
  8.1 9.8 copy-start.39
  8.1 9.8 copy-start.37
  9.5 10.4 collective-permute-start
  11.0 8.6 collective-permute-start.1
  12.4 7.1 collective-permute-start.2
  13.7 5.8 collective-permute-start.3
  19.8 3.7 copy-start.7
  19.8 3.7 copy-start.12
  19.8 3.7 copy-start.17
  23.5 6.6 copy-start.3
  23.5 3.0 copy-start.36
  30.2 131.1 %copy-start.38 = (s32[512]{0:T(512)S(1)}, s32[512]{0:T(512)}, u32[]{:S(2)}) copy-start(s32[512]{0:T(512)} %compare_select_fusion) | copy-start | bytes 6148
  30.2 222.9 %all-reduce.10.cloned.1.call-start = ((), (), s32[]{:S(2)}) async-start(), calls=%async_computation.1 | async-start | bytes 4194304 | tf_op jit(solution)/shard_map/psum | solution.py:84
  161.2 358.9 %all-reduce.12.cloned.1.call-start = ((), (), s32[]{:S(2)}) async-start(), calls=%async_computation.2 | async-start | bytes 4194304 | tf_op jit(solution)/shard_map/psum | solution.py:84
  297.3 22.7 %copy-start.4 = (f32[4,32,2048]{2,1,0:T(8,128)S(1)}, f32[4,32,2048]{2,1,0:T(8,128)}, u32[]{:S(2)}) copy-start(f32[4,32,2048]{2,1,0:T(8,128)} %copy-done.3) | copy-start | bytes 3145732
  297.3 22.7 %copy-start.8 = (f32[32,2048]{1,0:T(8,128)S(1)}, f32[32,2048]{1,0:T(8,128)}, u32[]{:S(2)}) copy-start(f32[32,2048]{1,0:T(8,128)} %copy-done.7) | copy-start | bytes 786436
  297.3 22.7 %copy-start.13 = (f32[32,2048]{1,0:T(8,128)S(1)}, f32[32,2048]{1,0:T(8,128)}, u32[]{:S(2)}) copy-start(f32[32,2048]{1,0:T(8,128)} %copy-done.12) | copy-start | bytes 786436
  297.3 22.7 %copy-start.18 = (f32[32,2048]{1,0:T(8,128)S(1)}, f32[32,2048]{1,0:T(8,128)}, u32[]{:S(2)}) copy-start(f32[32,2048]{1,0:T(8,128)} %copy-done.17) | copy-start | bytes 786436
  299.9 20.1 %collective-permute-start.4 = (f32[4,1,2048]{2,1,0:T(1,128)S(1)}, f32[4,1,2048]{2,1,0:T(1,128)S(1)}, u32[]{:S(2)}, u32[]{:S(2)}) collective-permute-start(f32[4,1,2048]{2,1,0:T(1,128)S(1)} %get-tuple-element.24), channel_id=1, source_target_pairs={{8,0},{16,8},{24,16},{32,24},{40,32},{48,40},{56,48},{64,56},{72,6... | collective-permute-start | bytes 98312 | tf_op jit(solution)/shard_map/ppermute | solution.py:21
  311.6 8.4 collective-permute-start.5
  312.9 5.6 collective-permute-start.6
  314.2 5.8 collective-permute-start.7
  320.0 71.8 %copy-start.5 = (f32[4,32,2048]{2,1,0:T(8,128)S(1)}, f32[4,32,2048]{2,1,0:T(8,128)}, u32[]{:S(2)}) copy-start(f32[4,32,2048]{2,1,0:T(8,128)} %copy-done.3) | copy-start | bytes 3145732
  400.2 211.8 %all-reduce.14.cloned.1.call-start = ((), (), s32[]{:S(2)}) async-start(), calls=%async_computation.3 | async-start | bytes 4194304 | tf_op jit(solution)/shard_map/psum | solution.py:84
  520.1 435.4 %all-reduce.16.cloned.1.call-start = ((), (), s32[]{:S(2)}) async-start(), calls=%async_computation.4 | async-start | bytes 4194304 | tf_op jit(solution)/shard_map/psum | solution.py:84
  652.7 10.1 copy-start.6
  662.8 75.3 %copy-start.44 = (f32[4]{0:T(128)S(1)}, f32[4]{0:T(128)}, u32[]{:S(2)}) copy-start(f32[4]{0:T(128)} %get-tuple-element.5) | copy-start | bytes 52
  738.1 11.7 copy-start.9
  738.1 11.7 copy-start.14
  738.1 11.7 copy-start.19
  740.1 8.5 collective-permute-start.8
  740.8 7.8 collective-permute-start.9
  742.0 5.3 collective-permute-start.10
  743.3 5.3 collective-permute-start.11
  835.8 211.6 %all-reduce.18.cloned.1.call-start = ((), (), s32[]{:S(2)}) async-start(), calls=%async_computation.5 | async-start | bytes 4194304 | tf_op jit(solution)/shard_map/psum | solution.py:84
  1098.2 75.7 %copy-start.43 = (f32[4]{0:T(128)S(1)}, f32[4]{0:T(128)}, u32[]{:S(2)}) copy-start(f32[4]{0:T(128)} %copy-done.42) | copy-start | bytes 52
  1173.9 11.7 copy-start.10
  1173.9 11.7 copy-start.15
  1173.9 11.7 copy-start.20
  1175.9 8.6 copy-start.22
  1175.9 82.3 %copy-start.41 = (f32[4]{0:T(128)S(1)}, f32[4]{0:T(128)}, u32[]{:S(2)}) copy-start(f32[4]{0:T(128)} %copy-done.40) | copy-start | bytes 52
  1175.9 8.5 collective-permute-start.12
  1176.7 7.8 collective-permute-start.13
  1177.8 5.3 collective-permute-start.14
  1179.1 5.3 collective-permute-start.15
  (19 other events, 29.9 us)
Sparse Core Ops, SparseCore 0:
  30.3 130.7 all-reduce.7
  163.7 89.4 all-reduce.9
  400.3 119.7 all-reduce.11
  522.5 89.4 all-reduce.13
  835.9 119.6 all-reduce.15
  957.9 89.4 all-reduce.17
